TPU v7x, 256 devices: a whole 4x4x8 slice. The times are simulated.
256 devices in a mesh: docs: 2 (over y_hi), ctx: 8 (over z), mp: 16 (over y_lo, x, core).
Axes of the slice: x: 4, y: 4 (y_hi: 2, y_lo: 2; y = y_hi * 2 + y_lo), z: 8, core: 2. Of those that a mesh axis runs over, the one named last changes fastest.
Arguments:
- residual_in: bfloat16 [8192, 5376], P(('docs', 'ctx', 'mp')), parts along dimension 0, may hold values from -15 to 15
- document_start: int32 [8192], P(('docs', 'ctx')), parts along dimension 0, may hold values from 0 to 3584, as said below
- input_gain: float32 [5376], replicated, may hold values from 0.25 to 1.75
- query_weight: bfloat16 [5376, 4096], P(None, 'mp'), may hold values from -0.078125 to 0.078125
- key_weight: bfloat16 [5376, 2048], P(None, 'mp'), may hold values from -0.078125 to 0.078125
- value_weight: bfloat16 [5376, 2048], P(None, 'mp'), may hold values from -0.078125 to 0.078125
- query_gain: float32 [128], replicated, may hold values from 0.6 to 20
- key_gain: float32 [128], replicated, may hold values from 0.6 to 20
- output_weight: bfloat16 [4096, 5376], P('mp'), may hold values from -0.09375 to 0.09375
- post_gain: float32 [5376], replicated, may hold values from 0.25 to 1.75
Outputs:
- residual_out: bfloat16 [8192, 5376], P(('docs', 'ctx', 'mp')), parts along dimension 0
There are 2 independent parts, one for each index of `docs`. A program takes and returns all parts, laid end to end along the dimension named above; an argument that names none is the same for every part. Nothing has to cross between parts.
Inputs may be any that keep to these rules, and one draw needn't show every extreme that they name: `document_start`: each entry is the index of the first token of that token's document; the documents lie end to end, there are 4 of them, one has exactly 3072 tokens, and the last has exactly 512 tokens.
All inputs are finite; a program needn't handle non-finite values.
Results may differ from a plain program's by a relative error of at most 0.014.
The roundings to bfloat16 on the way count: a program that leaves them out, or rounds other values in their place, can miss the bound.
Values may be sent and summed in bfloat16 or wider, within the bound.
No kernel may reach another device: no remote copies, remote signals or barrier semaphores. Data moves between devices by JAX's collectives and lax.ppermute only.
A program may use at most 64 MiB of HBM per device.

v0:
```python
import math
import jax
import jax.numpy as jnp
from jax import lax
from jax.sharding import PartitionSpec as P

query_scalar = 168.0
rope_base = 1000000.0
rope_factor = 8.0
epsilon = 1e-06


def make_angles(positions, head_size):
    frequency = rope_base ** (-(jnp.arange(head_size // 2, dtype=jnp.float32) * 2.0 / head_size))
    return (positions.astype(jnp.float32) / rope_factor)[:, None] * frequency[None, :]


def norm_rotate(values, head_gain, angles, head_count):
    tokens_here = values.shape[0]
    head_size = head_gain.shape[0]
    shaped = values.reshape(tokens_here, head_count, head_size)
    scaled = (
        shaped * lax.rsqrt(jnp.mean(shaped * shaped, axis=-1, keepdims=True) + epsilon) * head_gain
    )
    half_size = head_size // 2
    first_half = scaled[..., :half_size]
    second_half = scaled[..., half_size:]
    cosine = jnp.cos(angles)[:, None, :]
    sine_values = jnp.sin(angles)[:, None, :]
    rotated = jnp.concatenate(
        [
            first_half * cosine - second_half * sine_values,
            second_half * cosine + first_half * sine_values,
        ],
        axis=-1,
    )
    return rotated.astype(jnp.bfloat16)


def block_step(query_block, carried, key_piece, value_piece, key_index, first_row, piece_rows):
    queries, query_index, query_start = query_block

    def compute(running):
        running_max, running_total, accumulated = running
        scores = jnp.einsum(
            "tkgd,nkd->tkgn", queries, key_piece, preferred_element_type=jnp.float32
        ) / math.sqrt(query_scalar)
        allowed = (key_index[None, :] >= query_start[:, None]) & (
            key_index[None, :] <= query_index[:, None]
        )
        allowed = allowed[:, None, None, :]
        masked = jnp.where(allowed, scores, -1e30)
        new_max = jnp.maximum(running_max, jnp.max(masked, axis=-1))
        weights = jnp.where(allowed, jnp.exp(masked - new_max[..., None]), 0.0)
        new_total = jnp.sum(weights, axis=-1)
        product = jnp.einsum(
            "tkgn,nkd->tkgd",
            weights.astype(jnp.bfloat16),
            value_piece,
            preferred_element_type=jnp.float32,
        )
        return (new_max, new_total, product)

    def keep(running):
        return running

    is_live = (first_row <= jnp.max(query_index)) & (
        first_row + piece_rows - 1 >= jnp.min(query_start)
    )
    return lax.cond(is_live, compute, keep, carried)


def attend(query_blocks, key_rows, value_rows):
    initial = []
    for query_block in query_blocks:
        query_rows, kv_count, group_size, head_size = query_block[0].shape
        initial.append(
            (
                jnp.full((query_rows, kv_count, group_size), -1e30, jnp.float32),
                jnp.zeros((query_rows, kv_count, group_size), jnp.float32),
                jnp.zeros((query_rows, kv_count, group_size, head_size), jnp.float32),
            )
        )
    carried = tuple(initial)
    first_row = jnp.int32(0)
    key_piece = lax.all_gather(key_rows, "ctx", axis=0, tiled=True)
    value_piece = lax.all_gather(value_rows, "ctx", axis=0, tiled=True)
    piece_rows = key_piece.shape[0]
    key_index = jnp.arange(piece_rows, dtype=jnp.int32)
    outcome = []
    for query_block, carry_block in zip(query_blocks, carried):
        outcome.append(
            block_step(
                query_block, carry_block, key_piece, value_piece, key_index, first_row, piece_rows
            )
        )
    finals = tuple(outcome)
    results = []
    for final_block in finals:
        running_max, running_total, accumulated = final_block
        query_rows = accumulated.shape[0]
        results.append(
            (accumulated / running_total[..., None]).reshape(query_rows, -1).astype(jnp.bfloat16)
        )
    return results[0]


def body(
    residual_in,
    document_start,
    input_gain,
    query_weight,
    key_weight,
    value_weight,
    query_gain,
    key_gain,
    output_weight,
    post_gain,
):
    head_size = query_gain.shape[0]
    gathered = lax.all_gather(residual_in, "mp", axis=0, tiled=True)
    local_tokens = gathered.shape[0]
    widened = gathered.astype(jnp.float32)
    normed = (
        widened
        * lax.rsqrt(jnp.mean(widened * widened, axis=-1, keepdims=True) + epsilon)
        * input_gain
    ).astype(jnp.bfloat16)
    query_raw = jnp.dot(normed, query_weight, preferred_element_type=jnp.float32)
    key_raw = jnp.dot(normed, key_weight, preferred_element_type=jnp.float32)
    value_rows = jnp.dot(normed, value_weight, preferred_element_type=jnp.float32).astype(
        jnp.bfloat16
    )
    query_count = query_weight.shape[1] // head_size
    kv_count = key_weight.shape[1] // head_size
    group_size = query_count // kv_count
    block_index = lax.axis_index("ctx")
    positions = block_index * local_tokens + jnp.arange(local_tokens, dtype=jnp.int32)
    angles = make_angles(positions - document_start, head_size)
    query_rot = norm_rotate(query_raw, query_gain, angles, query_count).reshape(
        local_tokens, kv_count, group_size, head_size
    )
    key_rot = norm_rotate(key_raw, key_gain, angles, kv_count)
    value_heads = value_rows.reshape(local_tokens, kv_count, head_size)
    attended = attend([(query_rot, positions, document_start)], key_rot, value_heads)
    summed = lax.psum_scatter(
        jnp.dot(attended, output_weight, preferred_element_type=jnp.float32).astype(jnp.bfloat16),
        "mp",
        scatter_dimension=0,
        tiled=True,
    ).astype(jnp.float32)
    branch = (
        summed * lax.rsqrt(jnp.mean(summed * summed, axis=-1, keepdims=True) + epsilon) * post_gain
    )
    return (residual_in.astype(jnp.float32) + branch).astype(jnp.bfloat16)


def solution(mesh):
    return jax.shard_map(
        body,
        mesh=mesh,
        in_specs=(
            P(("docs", "ctx", "mp"), None),
            P(("docs", "ctx")),
            P(),
            P(None, "mp"),
            P(None, "mp"),
            P(None, "mp"),
            P(),
            P(),
            P("mp", None),
            P(),
        ),
        out_specs=P(("docs", "ctx", "mp"), None),
        check_vma=False,
    )
```

profile of v0, /device:TPU:32, one launch (start us, length us, event | category | flops | bytes accessed | tf_op | source)
XLA Modules:
  0.0 245.3 jit_solution(6276417553406046301)
XLA Ops:
  6.5 0.7 all-gather.5.cloned.1.call-update
  7.3 47.2 %all-gather.5.cloned.1.call-done = bf16[512,5376]{1,0:T(8,128)(2,1)} async-done(((bf16[32,5376]{1,0:T(8,128)(2,1)}), bf16[512,5376]{1,0:T(8,128)(2,1)}) %all-gather.5.cloned.1.call-update) | async-done | bytes 5505040 | tf_op jit(solution)/shard_map/all_gather | solution.py:121
  54.5 3.9 %fusion.17 = f32[512]{0:T(512)S(1)} fusion(bf16[512,5376]{1,0:T(8,128)(2,1)} %all-gather.5.cloned.1.call-done), kind=kLoop, calls=%fused_computation.20 | loop fusion | flops 8257024 | bytes 5507072 | tf_op jit(solution)/shard_map/reduce_sum | solution.py:126
  58.3 0.3 copy-done.2
  58.6 1.9 fusion.19
  60.5 2.4 copy-done.1
  62.9 2.3 convolution_convert_fusion.1
  65.3 4.9 %multiply_reduce_fusion.1 = (f32[512]{0:T(512)S(1)}, f32[512,128]{0,1:T(8,128)S(1)}) fusion(bf16[512,5376]{1,0:T(8,128)(2,1)} %copy-done.1, bf16[5376,128]{1,0:T(8,128)(2,1)} %param.16), kind=kOutput, calls=%fused_computation.42 | convolution fusion | flops 704773632 | bytes 7145472 | tf_op jit(solution)/shard_map/dot_general | solution.py:130
  70.3 0.1 multiply_bitcast_fusion
  70.4 0.6 fusion.31
  70.9 0.7 pad_maximum_fusion.1
  71.7 0.6 fusion.34
  72.3 0.7 reduce_min.9
  74.3 0.6 iota_add_fusion
  74.9 1.7 multiply_cosine_fusion
  76.6 5.9 %multiply_reduce_fusion = (f32[512,2]{0,1:T(2,128)S(1)}, f32[512,256]{0,1:T(8,128)}) fusion(bf16[512,5376]{1,0:T(8,128)(2,1)} %copy-done.1, bf16[5376,256]{1,0:T(8,128)(2,1)} %param.15), kind=kOutput, calls=%fused_computation.35 | convolution fusion | flops 1409547264 | bytes 8785920 | tf_op jit(solution)/shard_map/dot_general | solution.py:129
  82.5 1.2 copy.21
  83.7 0.2 multiply_multiply_fusion
  83.9 1.2 fusion.24
  85.1 0.1 pad_maximum_fusion
  85.3 17.8 %all-gather.9.cloned.1.call-done = bf16[4096,128]{1,0:T(8,128)(2,1)} async-done(((bf16[512,128]{1,0:T(8,128)(2,1)}), bf16[4096,128]{1,0:T(8,128)(2,1)}) %all-gather.9.cloned.1.call-update) | async-done | bytes 1048592 | tf_op jit(solution)/shard_map/all_gather | solution.py:87
  103.1 39.0 %all-gather.7.cloned.1.call-done = bf16[4096,1,128]{0,2,1:T(8,128)(2,1)} async-done(((bf16[512,1,128]{0,2,1:T(8,128)(2,1)}), bf16[4096,1,128]{0,2,1:T(8,128)(2,1)}) %all-gather.7.cloned.1.call-update) | async-done | bytes 1048592 | tf_op jit(solution)/shard_map/all_gather | solution.py:86
  142.2 18.4 %conditional.1 = (f32[512,1,2]{0,2,1:T(2,128)S(1)}, f32[512,1,2,128]{0,3,2,1:T(8,128)S(1)}) conditional(s32[]{:T(128)} %convert_element_type.54, () %tuple.13, (s32[4096]{0:T(1024)S(1)}, s32[4096]{0:T(1024)S(1)}, s32[512]{0:T(512)}, s32[512]{0:T(512)}, bf16[4096,1,128]{0,2,1:T(8,128)(2,1)}, /*index=5*/bf16[512,1,2,128]{3,0,2,1:T(8,128)(2,1)S(1)}, ...), branch_computations={%region_5.0_spmd, %region_6.9_spmd} | conditional | flops 2208300032 | bytes 65859628 | solution.py:70
  142.2 3.8 %compare_and_fusion = pred[512,4096]{0,1:T(8,128)(4,1)S(1)} fusion(s32[512]{0:T(512)} %get-tuple-element.21, s32[512]{0:T(512)} %get-tuple-element.19, s32[4096]{0:T(1024)S(1)} %get-tuple-element.20, s32[4096]{0:T(1024)S(1)} %get-tuple-element.20), kind=kLoop, calls=%fused_computation.8 | loop fusion | flops 6291456 | bytes 2134016 | tf_op jit(solution)/shard_map/cond/branch_1_fun/and | solution.py:48
  146.0 5.2 %fusion = (f32[512,2]{0,1:T(2,128)S(1)}, f32[4096,512,2]{1,0,2:T(8,128)S(1)}) fusion(pred[512,4096]{0,1:T(8,128)(4,1)S(1)} %compare_and_fusion, bf16[512,1,2,128]{3,0,2,1:T(8,128)(2,1)S(1)} %get-tuple-element.23, bf16[4096,1,128]{0,2,1:T(8,128)(2,1)} %get-tuple-element.47), kind=kOutput, calls=%fused_computation.2 | convolution fusion | flops 1086323712 | bytes 20189184 | tf_op jit(solution)/shard_map/cond/branch_1_fun/tkgd,nkd->tkgn/dot_general | solution.py:45
  151.2 5.0 %fusion.7 = f32[512,1,2,128]{0,3,2,1:T(8,128)S(1)} fusion(f32[4096,512,2]{1,0,2:T(8,128)S(1)} %get-tuple-element.52, f32[512,2]{0,1:T(2,128)S(1)} %broadcast_maximum_fusion, pred[512,4096]{0,1:T(8,128)(4,1)S(1)} %compare_and_fusion, bf16[4096,1,128]{2,0,1:T(8,128)(2,1)S(1)} %copy-done.10), kind=kOutput, calls=%fused_computation.9 | convolution fusion | flops 1094713344 | bytes 20451328 | tf_op jit(solution)/shard_map/cond/branch_1_fun/tkgn,nkd->tkgd/dot_general | solution.py:56
  156.1 4.4 %fusion.2 = f32[512,2]{0,1:T(2,128)S(1)} fusion(f32[4096,512,2]{1,0,2:T(8,128)S(1)} %get-tuple-element.52, f32[512,2]{0,1:T(2,128)S(1)} %broadcast_maximum_fusion, pred[512,4096]{0,1:T(8,128)(4,1)S(1)} %compare_and_fusion), kind=kLoop, calls=%fused_computation.4 | loop fusion | flops 20970496 | bytes 18882560 | tf_op jit(solution)/shard_map/cond/branch_1_fun/reduce_sum | solution.py:55
  160.6 0.1 divide_convert_fusion
  160.7 4.0 %convolution_convert_fusion = bf16[512,5376]{1,0:T(8,128)(2,1)} fusion(bf16[512,256]{0,1:T(8,128)(2,1)S(1)} %bitcast.65, bf16[256,5376]{1,0:T(8,128)(2,1)S(1)} %copy-done), kind=kOutput, calls=%fused_computation.23 | convolution fusion | flops 1412038656 | bytes 8519680 | tf_op jit(solution)/shard_map/dot_general | solution.py:147
  164.8 70.9 %reduce-scatter.2.cloned.1.call-done = bf16[32,5376]{1,0:T(8,128)(2,1)} async-done(((bf16[512,5376]{1,0:T(8,128)(2,1)}), bf16[32,5376]{1,0:T(8,128)(2,1)}) %reduce-scatter.2.cloned.1.call-update) | async-done | bytes 344080 | tf_op jit(solution)/shard_map/reduce_scatter | solution.py:146
  235.7 1.2 fusion.20
  236.9 1.9 fusion.23
  (35 shorter events, 0.3 us)
Async XLA Ops:
  6.5 154.1 %copy-start = (bf16[256,5376]{1,0:T(8,128)(2,1)S(1)}, bf16[256,5376]{1,0:T(8,128)(2,1)}, u32[]{:S(2)}) copy-start(bf16[256,5376]{1,0:T(8,128)(2,1)} %param.20) | copy-start | bytes 8257540
  6.5 51.8 %copy-start.5 = (f32[5376]{0:T(1024)S(1)}, f32[5376]{0:T(1024)}, u32[]{:S(2)}) copy-start(f32[5376]{0:T(1024)} %param.14) | copy-start | bytes 64516
  6.5 47.9 %all-gather.5.cloned.1.call-start = ((), (), s32[]{:S(2)}) async-start(), calls=%async_computation.1 | async-start | bytes 5849088 | tf_op jit(solution)/shard_map/all_gather | solution.py:121
  7.3 95.9 %all-gather.9.cloned.1.call-start = ((), (), s32[]{:S(2)}) async-start(), calls=%async_computation.4 | async-start | bytes 1179648 | tf_op jit(solution)/shard_map/all_gather | solution.py:87
  54.5 4.2 %copy-start.2 = (bf16[512,5376]{1,0:T(8,128)(2,1)S(1)}, bf16[512,5376]{1,0:T(8,128)(2,1)}, u32[]{:S(2)}) copy-start(bf16[512,5376]{1,0:T(8,128)(2,1)} %all-gather.5.cloned.1.call-done) | copy-start | bytes 16515076
  58.6 4.3 %copy-start.9 = (bf16[5376,128]{1,0:T(8,128)(2,1)S(1)}, bf16[5376,128]{1,0:T(8,128)(2,1)}, u32[]{:S(2)}) copy-start(bf16[5376,128]{1,0:T(8,128)(2,1)} %param.17) | copy-start | bytes 4128772
  60.5 2.4 copy-start.1
  62.9 2.4 copy-start.6
  65.2 5.1 %copy-start.7 = (f32[128]{0:T(128)S(1)}, f32[128]{0:T(128)}, u32[]{:S(2)}) copy-start(f32[128]{0:T(128)} %param.19) | copy-start | bytes 1540
  65.2 77.0 %all-gather.7.cloned.1.call-start = ((), (), s32[]{:S(2)}) async-start(), calls=%async_computation.2 | async-start | bytes 1179648 | tf_op jit(solution)/shard_map/all_gather | solution.py:86
  71.6 164.1 %reduce-scatter.2.cloned.1.call-start = ((), (), s32[]{:S(2)}) async-start(), calls=%async_computation.3 | async-start | bytes 5849088 | tf_op jit(solution)/shard_map/reduce_scatter | solution.py:146
  76.6 7.1 %copy-start.8 = (f32[128]{0:T(128)S(1)}, f32[128]{0:T(128)}, u32[]{:S(2)}) copy-start(f32[128]{0:T(128)} %param.18) | copy-start | bytes 1540
  146.0 5.2 %copy-start.10 = (bf16[4096,1,128]{2,0,1:T(8,128)(2,1)S(1)}, bf16[4096,1,128]{2,0,1:T(8,128)(2,1)}, u32[]{:S(2)}) copy-start(bf16[4096,1,128]{2,0,1:T(8,128)(2,1)} %get-tuple-element.24) | copy-start | bytes 3145732 | tf_op jit(solution)/shard_map/cond
  160.7 76.2 %copy-start.3 = (bf16[32,5376]{1,0:T(8,128)(2,1)S(1)}, bf16[32,5376]{1,0:T(8,128)(2,1)}, u32[]{:S(2)}) copy-start(bf16[32,5376]{1,0:T(8,128)(2,1)} %param.12) | copy-start | bytes 1032196
  160.7 76.2 %copy-start.4 = (f32[5376]{0:T(1024)S(1)}, f32[5376]{0:T(1024)}, u32[]{:S(2)}) copy-start(f32[5376]{0:T(1024)} %param.21) | copy-start | bytes 64516
Sparse Core Ops, SparseCore 0:
  9.2 45.2 all-gather.4
  65.3 37.7 all-gather.8
  104.9 37.1 all-gather.6
  164.9 70.7 reduce-scatter.1
where the time goes:
time: 246 us; the launch traced here: 245 us
  waiting for transfers between devices  176 us (72%)
  matrix products  27.2 us (11%)
  other arithmetic  23.6 us (10%)
  between operations  14.6 us (6%)
  local copies, waits for them, and re-layouts  3.97 us (2%)
    reduce_scatter x1, waiting for transfers between devices, body(): lax.psum_scatter(jnp.dot(attended, output_weight, preferred_element_type=...  70.9 us
    all_gather x1, waiting for transfers between devices, body(): gathered = lax.all_gather(residual_in, 'mp', axis=0, tiled=True)  47.2 us
    all_gather x1, waiting for transfers between devices, attend(): key_piece = lax.all_gather(key_rows, 'ctx', axis=0, tiled=True)  39 us
    all_gather x1, waiting for transfers between devices, attend(): value_piece = lax.all_gather(value_rows, 'ctx', axis=0, tiled=True)  17.8 us
    dot_general x1, matrix products, body(): jnp.dot(normed, query_weight, preferred_element_type=jnp.float32)  5.87 us
    dot_general x1, matrix products, compute(): jnp.einsum('tkgd,nkd->tkgn', queries, key_piece, preferred_element_type=j...  5.17 us
    dot_general x1, matrix products, compute(): jnp.einsum('tkgn,nkd->tkgd', weights.astype(jnp.bfloat16), value_piece, p...  4.97 us
    dot_general x1, matrix products, body(): key_raw = jnp.dot(normed, key_weight, preferred_element_type=jnp.float32)  4.92 us
  transfers between devices with their start and end apart: 4, of which 4 were waited for; matrix products, arithmetic and copies ran while one was open for 8% of the time, Pallas kernels for 0%

commit v1 on v0

--- a/solution.py
+++ b/solution.py
@@ -83,8 +83,11 @@
         )
     carried = tuple(initial)
     first_row = jnp.int32(0)
-    key_piece = lax.all_gather(key_rows, "ctx", axis=0, tiled=True)
-    value_piece = lax.all_gather(value_rows, "ctx", axis=0, tiled=True)
+    key_piece, value_piece = jnp.split(
+        lax.all_gather(jnp.concatenate([key_rows, value_rows], axis=1), "ctx", axis=0, tiled=True),
+        [key_rows.shape[1]],
+        axis=1,
+    )
     piece_rows = key_piece.shape[0]
     key_index = jnp.arange(piece_rows, dtype=jnp.int32)
     outcome = []

time: 246 us -> 216 us (0.88)
  waiting for transfers between devices: 176 us -> 145 us
  matrix products: 27.2 us -> 23 us
  other arithmetic: 23.6 us -> 26.9 us
    all_gather x2 -> x1, waiting for transfers between devices: 56.9 us -> 27 us  [attend(): lax.all_gather(jnp.concatenate([key_rows, value_rows], axis=1), 'ctx', ax...]
    another operation x0 -> x1, local copies, waits for them, and re-layouts: none -> 4.08 us
    dot_general x1, matrix products: 4.92 us -> 1.95 us  [body(): key_raw = jnp.dot(normed, key_weight, preferred_element_type=jnp.float32)]
  transfers between devices with their start and end apart: 4 -> 3, of which waited for: 4 -> 3; matrix products, arithmetic and copies ran while one was open for 8% -> 6% of each run, Pallas kernels for 0% -> 0%
where the time goes in v1:
time: 216 us
  waiting for transfers between devices  145 us (67%)
  other arithmetic  26.9 us (12%)
  matrix products  23 us (11%)
  between operations  14.6 us (7%)
  local copies, waits for them, and re-layouts  6.07 us (3%)
    reduce_scatter x1, waiting for transfers between devices, body(): lax.psum_scatter(jnp.dot(attended, output_weight, preferred_element_type=...  70.8 us
    all_gather x1, waiting for transfers between devices, body(): gathered = lax.all_gather(residual_in, 'mp', axis=0, tiled=True)  46.4 us
    all_gather x1, waiting for transfers between devices, attend(): lax.all_gather(jnp.concatenate([key_rows, value_rows], axis=1), 'ctx', ax...  27 us
    dot_general x1, matrix products, body(): jnp.dot(normed, query_weight, preferred_element_type=jnp.float32)  5.85 us
    dot_general x1, matrix products, compute(): jnp.einsum('tkgd,nkd->tkgn', queries, key_piece, preferred_element_type=j...  5.27 us
    reduce_sum x1, other arithmetic, compute(): new_total = jnp.sum(weights, axis=-1)  5.04 us
    and x1, other arithmetic, compute(): (key_index[None, :] >= query_start[:, None]) & (key_index[None, :] <= que...  4.92 us
  transfers between devices with their start and end apart: 3, of which 3 were waited for; matrix products, arithmetic and copies ran while one was open for 6% of the time, Pallas kernels for 0%

profile of v1, /device:TPU:32, one launch (start us, length us, event | category | flops | bytes accessed | tf_op | source)
XLA Modules:
  0.0 215.6 jit_solution(9896693661496474076)
XLA Ops:
  6.5 0.7 all-gather.3.cloned.1.call-update
  7.3 0.7 convert_multiply_fusion.4
  8.1 46.4 %all-gather.3.cloned.1.call-done = bf16[512,5376]{1,0:T(8,128)(2,1)} async-done(((bf16[32,5376]{1,0:T(8,128)(2,1)}), bf16[512,5376]{1,0:T(8,128)(2,1)}) %all-gather.3.cloned.1.call-update) | async-done | bytes 5505040 | tf_op jit(solution)/shard_map/all_gather | solution.py:124
  54.5 3.9 %fusion.15 = f32[512]{0:T(512)S(1)} fusion(bf16[512,5376]{1,0:T(8,128)(2,1)} %all-gather.3.cloned.1.call-done), kind=kLoop, calls=%fused_computation.20 | loop fusion | flops 8257024 | bytes 5507072 | tf_op jit(solution)/shard_map/reduce_sum | solution.py:129
  58.3 0.3 copy-done.2
  58.6 1.9 fusion.17
  60.6 1.9 fusion.18
  62.5 0.4 copy-done.7
  62.9 2.0 multiply_reduce_fusion.1
  65.0 0.6 fusion.30
  65.6 0.7 pad_maximum_fusion
  66.4 0.7 fusion.33
  67.1 0.7 reduce_min.9
  69.0 0.6 iota_add_fusion
  69.6 1.8 multiply_cosine_fusion
  71.3 5.9 %multiply_reduce_fusion = (f32[512,2]{0,1:T(2,128)S(1)}, f32[512,256]{0,1:T(8,128)}) fusion(bf16[512,5376]{1,0:T(8,128)(2,1)} %copy-done.1, bf16[5376,256]{1,0:T(8,128)(2,1)} %param.15), kind=kOutput, calls=%fused_computation.36 | convolution fusion | flops 1409547264 | bytes 8785920 | tf_op jit(solution)/shard_map/dot_general | solution.py:132
  77.2 1.2 copy.24
  78.5 0.2 multiply_multiply_fusion
  78.7 1.2 fusion.23
  79.9 0.1 pad_maximum_fusion.1
  80.0 27.0 %all-gather.5.cloned.1.call-done = bf16[4096,2,128]{0,2,1:T(8,128)(2,1)} async-done(((bf16[512,2,128]{0,2,1:T(8,128)(2,1)}), bf16[4096,2,128]{0,2,1:T(8,128)(2,1)}) %all-gather.5.cloned.1.call-update) | async-done | bytes 2097168 | tf_op jit(solution)/shard_map/all_gather | solution.py:87
  107.0 23.4 %conditional.1 = (f32[512,1,2]{0,2,1:T(2,128)}, f32[512,1,2,128]{0,3,2,1:T(8,128)S(1)}) conditional(s32[]{:T(128)} %convert_element_type.54, () %tuple.13, (s32[4096]{0:T(1024)S(1)}, s32[4096]{0:T(1024)S(1)}, s32[512]{0:T(512)}, s32[512]{0:T(512)}, bf16[4096,2,128]{0,2,1:T(8,128)(2,1)}, /*index=5*/bf16[512,1,2,128]{3,0,2,1:T(8,128)(2,1)S(1)}) %tuple.14), branch_computations={%region_5.0_spmd, %region_6.9_spmd} | conditional | flops 2208300032 | bytes 82636872 | solution.py:70
  107.0 4.9 %compare_and_fusion = pred[512,4096]{0,1:T(8,128)(4,1)} fusion(s32[512]{0:T(512)} %get-tuple-element.22, s32[512]{0:T(512)} %get-tuple-element.20, s32[4096]{0:T(1024)S(1)} %get-tuple-element.21, s32[4096]{0:T(1024)S(1)} %get-tuple-element.21), kind=kLoop, calls=%fused_computation.8 | loop fusion | flops 6291456 | bytes 2134016 | tf_op jit(solution)/shard_map/cond/branch_1_fun/and | solution.py:48
  112.0 4.1 %copy.25 = bf16[4096,2,128]{2,0,1:T(8,128)(2,1)} copy(bf16[4096,2,128]{0,2,1:T(8,128)(2,1)} %get-tuple-element.45) | data formatting | bytes 4194304 | tf_op jit(solution)/shard_map
  116.0 5.3 %fusion = (f32[512,2]{0,1:T(2,128)S(1)}, f32[4096,512,2]{1,0,2:T(8,128)S(1)}) fusion(pred[512,4096]{0,1:T(8,128)(4,1)} %compare_and_fusion, bf16[512,1,2,128]{3,0,2,1:T(8,128)(2,1)S(1)} %get-tuple-element.24, bf16[4096,2,128]{2,0,1:T(8,128)(2,1)} %copy.25), kind=kOutput, calls=%fused_computation.2 | convolution fusion | flops 1086323712 | bytes 20189184 | tf_op jit(solution)/shard_map/cond/branch_1_fun/tkgd,nkd->tkgn/dot_general | solution.py:45
  121.4 4.0 %fusion.7 = f32[512,1,2,128]{0,3,2,1:T(8,128)S(1)} fusion(f32[4096,512,2]{1,0,2:T(8,128)S(1)} %get-tuple-element.49, f32[512,2]{0,1:T(2,128)S(1)} %broadcast_maximum_fusion, pred[512,4096]{0,1:T(8,128)(4,1)S(1)} %copy-done.3, bf16[4096,2,128]{2,0,1:T(8,128)(2,1)S(1)} %copy-done.4), kind=kOutput, calls=%fused_computation.9 | convolution fusion | flops 1094713344 | bytes 20451328 | tf_op jit(solution)/shard_map/cond/branch_1_fun/tkgn,nkd->tkgd/dot_general | solution.py:56
  125.4 5.0 %fusion.2 = f32[512,2]{0,1:T(2,128)} fusion(f32[4096,512,2]{1,0,2:T(8,128)S(1)} %get-tuple-element.49, f32[512,2]{0,1:T(2,128)S(1)} %broadcast_maximum_fusion, pred[512,4096]{0,1:T(8,128)(4,1)S(1)} %copy-done.3), kind=kLoop, calls=%fused_computation.4 | loop fusion | flops 20970496 | bytes 18882560 | tf_op jit(solution)/shard_map/cond/branch_1_fun/reduce_sum | solution.py:55
  130.4 0.7 divide_convert_fusion
  131.2 4.0 %convolution_convert_fusion = bf16[512,5376]{1,0:T(8,128)(2,1)} fusion(bf16[512,256]{0,1:T(8,128)(2,1)S(1)} %bitcast.65, bf16[256,5376]{1,0:T(8,128)(2,1)S(1)} %copy-done), kind=kOutput, calls=%fused_computation.23 | convolution fusion | flops 1412038656 | bytes 8519680 | tf_op jit(solution)/shard_map/dot_general | solution.py:150
  135.2 70.8 %reduce-scatter.2.cloned.1.call-done = bf16[32,5376]{1,0:T(8,128)(2,1)} async-done(((bf16[512,5376]{1,0:T(8,128)(2,1)}), bf16[32,5376]{1,0:T(8,128)(2,1)}) %reduce-scatter.2.cloned.1.call-update) | async-done | bytes 344080 | tf_op jit(solution)/shard_map/reduce_scatter | solution.py:149
  206.0 1.2 fusion.19
  207.2 1.9 fusion.22
  (37 shorter events, 0.3 us)
Async XLA Ops:
  6.5 124.6 %copy-start = (bf16[256,5376]{1,0:T(8,128)(2,1)S(1)}, bf16[256,5376]{1,0:T(8,128)(2,1)}, u32[]{:S(2)}) copy-start(bf16[256,5376]{1,0:T(8,128)(2,1)} %param.20) | copy-start | bytes 8257540
  6.5 51.8 %copy-start.9 = (f32[5376]{0:T(1024)S(1)}, f32[5376]{0:T(1024)}, u32[]{:S(2)}) copy-start(f32[5376]{0:T(1024)} %param.14) | copy-start | bytes 64516
  6.5 47.9 %all-gather.3.cloned.1.call-start = ((), (), s32[]{:S(2)}) async-start(), calls=%async_computation.1 | async-start | bytes 5849088 | tf_op jit(solution)/shard_map/all_gather | solution.py:124
  7.3 99.8 %all-gather.5.cloned.1.call-start = ((), (), s32[]{:S(2)}) async-start(), calls=%async_computation.2 | async-start | bytes 2359296 | tf_op jit(solution)/shard_map/all_gather | solution.py:87
  54.5 4.2 %copy-start.2 = (bf16[512,5376]{1,0:T(8,128)(2,1)S(1)}, bf16[512,5376]{1,0:T(8,128)(2,1)}, u32[]{:S(2)}) copy-start(bf16[512,5376]{1,0:T(8,128)(2,1)} %all-gather.3.cloned.1.call-done) | copy-start | bytes 16515076
  58.6 1.9 copy-start.5
  60.5 4.3 %copy-start.1 = (bf16[512,5376]{1,0:T(8,128)(2,1)}, bf16[512,5376]{1,0:T(8,128)(2,1)S(1)}, u32[]{:S(2)}) copy-start(bf16[512,5376]{1,0:T(8,128)(2,1)S(1)} %fusion.17) | copy-start | bytes 16515076
  60.5 2.4 %copy-start.7 = (bf16[5376,128]{1,0:T(8,128)(2,1)S(1)}, bf16[5376,128]{1,0:T(8,128)(2,1)}, u32[]{:S(2)}) copy-start(bf16[5376,128]{1,0:T(8,128)(2,1)} %param.16) | copy-start | bytes 4128772
  62.9 2.0 copy-start.11
  62.9 4.1 %copy-start.10 = (s32[512]{0:T(512)S(1)}, s32[512]{0:T(512)}, u32[]{:S(2)}) copy-start(s32[512]{0:T(512)} %param.13) | copy-start | bytes 6148
  66.3 139.7 %reduce-scatter.2.cloned.1.call-start = ((), (), s32[]{:S(2)}) async-start(), calls=%async_computation.3 | async-start | bytes 5849088 | tf_op jit(solution)/shard_map/reduce_scatter | solution.py:149
  71.3 7.1 %copy-start.12 = (f32[128]{0:T(128)S(1)}, f32[128]{0:T(128)}, u32[]{:S(2)}) copy-start(f32[128]{0:T(128)} %param.18) | copy-start | bytes 1540
  116.0 5.3 %copy-start.3 = (pred[512,4096]{0,1:T(8,128)(4,1)S(1)}, pred[512,4096]{0,1:T(8,128)(4,1)}, u32[]{:S(2)}) copy-start(pred[512,4096]{0,1:T(8,128)(4,1)} %compare_and_fusion) | copy-start | bytes 6291460 | tf_op jit(solution)/shard_map/cond
  116.0 5.3 %copy-start.4 = (bf16[4096,2,128]{2,0,1:T(8,128)(2,1)S(1)}, bf16[4096,2,128]{2,0,1:T(8,128)(2,1)}, u32[]{:S(2)}) copy-start(bf16[4096,2,128]{2,0,1:T(8,128)(2,1)} %copy.25) | copy-start | bytes 6291460 | tf_op jit(solution)/shard_map/cond
  131.1 76.1 %copy-start.6 = (bf16[32,5376]{1,0:T(8,128)(2,1)S(1)}, bf16[32,5376]{1,0:T(8,128)(2,1)}, u32[]{:S(2)}) copy-start(bf16[32,5376]{1,0:T(8,128)(2,1)} %param.12) | copy-start | bytes 1032196
  131.1 76.1 %copy-start.8 = (f32[5376]{0:T(1024)S(1)}, f32[5376]{0:T(1024)}, u32[]{:S(2)}) copy-start(f32[5376]{0:T(1024)} %param.21) | copy-start | bytes 64516
Sparse Core Ops, SparseCore 0:
  9.2 45.2 all-gather.2
  66.4 40.5 all-gather.4
  135.3 70.6 reduce-scatter.1
